TPU v7x, 32 devices: a whole 2x2x4 slice. The times are simulated.
32 devices in a mesh: req: 16 (over z, y, x), hist: 2 (over core).
Axes of the slice: x: 2, y: 2, z: 4, core: 2. Of those that a mesh axis runs over, the one named last changes fastest.
Arguments:
- cand_embed: bfloat16 [16, 768, 1024], P('req', 'hist'), may hold values from -6 to 6
- hist_keys: bfloat16 [16, 256, 1024], P('req', 'hist'), may hold values from -6 to 6
- hist_values: bfloat16 [16, 256, 1024], P('req', 'hist'), may hold values from -6 to 6
- in_weight: bfloat16 [1024, 4096], P('req'), may hold values from -0.1875 to 0.1875
- out_weight: bfloat16 [1024, 1024], replicated, may hold values from -0.1875 to 0.1875
- norm_gain: float32 [1024], replicated, may hold values from 0.25 to 1.75
- cand_counts: int32 [16], P('req'), may hold values from 96 to 768, as said below
- hist_lengths: int32 [16], P('req'), may hold values from 128 to 256, as said below
- self_mask: int32 [16, 768, 64], P('req', 'hist'), may hold values 0 or 1
Outputs:
- cand_out: bfloat16 [16, 768, 1024], P('req', 'hist')
Inputs may be any that keep to these rules, and one draw needn't show every extreme that they name: `cand_counts`: in every draw one request has all 768 candidate slots live; the others have between 96 and 256. `hist_lengths`: multiples of 128; in every draw one request has the full 256.
All inputs are finite; a program needn't handle non-finite values. No bound on the sum of `self_mask` on one device may be relied on, other than what follows from the above.
Results may differ from a plain program's by a relative error of at most 0.0027.
Values may be sent and summed in bfloat16 or wider, within the bound.
A program may use at most 128 MiB of HBM per device.

v0:
```python
import jax
import jax.numpy as jnp
from jax import lax
from jax.sharding import PartitionSpec as P

HEADS = 8
SELF_BLOCK = 64


def on_device(
    cand_embed,
    hist_keys,
    hist_values,
    in_weight,
    out_weight,
    norm_gain,
    cand_counts,
    hist_lengths,
    self_mask,
):
    req_count, cand_count, model_width = cand_embed.shape
    head_dim = model_width // HEADS
    scale_factor = head_dim ** (-0.5)
    flat_rows = cand_embed.reshape(req_count * cand_count, model_width)
    pre_act = jnp.dot(
        flat_rows,
        lax.all_gather(in_weight, "req", axis=0, tiled=True),
        preferred_element_type=jnp.float32,
    )
    projected = (
        jax.nn.silu(pre_act).astype(jnp.bfloat16).reshape(req_count, cand_count, 4 * model_width)
    )
    gate_u = projected[:, :, :model_width]
    self_values = projected[:, :, model_width : 2 * model_width]
    queries = projected[:, :, 2 * model_width : 3 * model_width]
    self_keys = projected[:, :, 3 * model_width :]
    query_heads = queries.reshape(req_count, cand_count, HEADS, head_dim)
    divisor = (hist_lengths + SELF_BLOCK).astype(jnp.float32)
    cand_index = lax.axis_index("hist") * cand_count + jnp.arange(cand_count)
    is_live = cand_index[None, :] < cand_counts[:, None]
    key_part = lax.all_gather(hist_keys, "hist", axis=1, tiled=True)
    value_part = lax.all_gather(hist_values, "hist", axis=1, tiled=True)
    span = key_part.shape[1]
    key_heads = key_part.reshape(req_count, span, HEADS, head_dim)
    value_heads = value_part.reshape(req_count, span, HEADS, head_dim)
    scores = (
        jnp.einsum("rchd,rnhd->rhcn", query_heads, key_heads, preferred_element_type=jnp.float32)
        * scale_factor
    )
    visible = (jnp.arange(span)[None, :] < hist_lengths[:, None]).astype(jnp.float32)
    mixing = (
        jax.nn.silu(scores) * visible[:, None, None, :] / divisor[:, None, None, None]
    ).astype(jnp.bfloat16)
    attended = jnp.einsum(
        "rhcn,rnhd->rchd", mixing, value_heads, preferred_element_type=jnp.float32
    )
    blocks = cand_count // SELF_BLOCK
    query_blocks = queries.reshape(req_count, blocks, SELF_BLOCK, HEADS, head_dim)
    key_blocks = self_keys.reshape(req_count, blocks, SELF_BLOCK, HEADS, head_dim)
    value_blocks = self_values.reshape(req_count, blocks, SELF_BLOCK, HEADS, head_dim)
    self_scores = (
        jnp.einsum(
            "rbphd,rbchd->rbhpc", query_blocks, key_blocks, preferred_element_type=jnp.float32
        )
        * scale_factor
    )
    position = jnp.arange(SELF_BLOCK)
    causal = position[None, :] <= position[:, None]
    diagonal = position[None, :] == position[:, None]
    given = self_mask.reshape(req_count, blocks, SELF_BLOCK, SELF_BLOCK) == 1
    key_live = is_live.reshape(req_count, blocks, 1, SELF_BLOCK)
    allowed = (causal[None, None] & (given | diagonal[None, None]) & key_live).astype(jnp.float32)
    self_mix = (
        jax.nn.silu(self_scores) * allowed[:, :, None, :, :] / divisor[:, None, None, None, None]
    ).astype(jnp.bfloat16)
    self_part = jnp.einsum(
        "rbhpc,rbchd->rbphd", self_mix, value_blocks, preferred_element_type=jnp.float32
    )
    attended = (attended + self_part.reshape(req_count, cand_count, HEADS, head_dim)).reshape(
        req_count, cand_count, model_width
    )
    average = jnp.mean(attended, axis=2, keepdims=True)
    variance = jnp.mean((attended - average) ** 2, axis=2, keepdims=True)
    gated = (
        (attended - average) / jnp.sqrt(variance + 1e-05) * norm_gain * gate_u.astype(jnp.float32)
    ).astype(jnp.bfloat16)
    gated_rows = gated.reshape(req_count * cand_count, model_width)
    branch = jnp.dot(gated_rows, out_weight, preferred_element_type=jnp.float32)
    branch = branch.reshape(req_count, cand_count, model_width)
    result = cand_embed.astype(jnp.float32) + is_live.astype(jnp.float32)[:, :, None] * branch
    return result.astype(jnp.bfloat16)


def solution(mesh):
    in_specs = (
        P("req", "hist", None),
        P("req", "hist", None),
        P("req", "hist", None),
        P("req", None),
        P(),
        P(),
        P("req"),
        P("req"),
        P("req", "hist", None),
    )
    out_specs = P("req", "hist", None)
    return jax.shard_map(
        on_device, mesh=mesh, in_specs=in_specs, out_specs=out_specs, check_vma=False
    )
```

profile of v0, /device:TPU:0, one launch (start us, length us, event | category | flops | bytes accessed | tf_op | source)
XLA Modules:
  0.0 166.9 jit_solution(5197467183300313820)
XLA Ops:
  6.5 0.0 copy-start
  6.5 0.0 copy-start.2
  6.5 0.0 all-gather.2.cloned.1.call-start
  6.5 0.7 all-gather.2.cloned.1.call-update
  7.3 0.0 copy-start.3
  8.0 0.1 copy.35
  8.1 0.9 broadcast_compare_fusion
  9.0 0.1 eq.30
  9.2 0.1 and_convert_fusion
  9.3 0.8 copy.36
  10.8 0.0 copy-done.2
  10.8 2.3 %all_gather.11 = bf16[1,256,1024]{2,1,0:T(8,128)(2,1)S(1)} all-gather(bf16[1,128,1024]{2,1,0:T(8,128)(2,1)S(1)} %copy-done.2), channel_id=1, replica_groups=mesh['req'=16,'hist'=2] {'hist'}, dimensions={1}, use_global_device_ids=true | all-gather | bytes 786432 | tf_op jit(solution)/shard_map/all_gather | solution.py:42
  13.1 1.0 copy.32
  14.1 0.0 copy-done.3
  14.1 0.2 copy.29
  14.3 2.2 %all_gather.10 = bf16[1,256,1024]{1,2,0:T(8,128)(2,1)S(1)} all-gather(bf16[1,128,1024]{1,2,0:T(8,128)(2,1)S(1)} %copy.29), channel_id=1, replica_groups=mesh['req'=16,'hist'=2] {'hist'}, dimensions={1}, use_global_device_ids=true | all-gather | bytes 786432 | tf_op jit(solution)/shard_map/all_gather | solution.py:41
  16.5 109.2 %all-gather.2.cloned.1.call-done = bf16[1024,4096]{1,0:T(8,128)(2,1)} async-done(((bf16[64,4096]{1,0:T(8,128)(2,1)}), bf16[1024,4096]{1,0:T(8,128)(2,1)}) %all-gather.2.cloned.1.call-update) | async-done | bytes 8388624 | tf_op jit(solution)/shard_map/all_gather | solution.py:27
  125.7 7.5 %fusion = bf16[1,384,4096]{2,1,0:T(8,128)(2,1)S(1)} fusion(bf16[1024,4096]{1,0:T(8,128)(2,1)} %all-gather.2.cloned.1.call-done, bf16[1,384,1024]{2,1,0:T(8,128)(2,1)} %param.9), kind=kOutput, calls=%fused_computation.2 | convolution fusion | flops 3229089792 | bytes 12320768 | tf_op jit(solution)/shard_map/dot_general | solution.py:25
  133.2 0.0 copy-start.1
  133.2 0.5 slice_bitcast_fusion.2
  133.7 1.1 copy-done.1
  134.8 0.2 copy.43
  135.0 1.1 copy.45
  136.1 1.1 copy.46
  137.2 3.7 %convolution_bitcast_fusion = f32[1,6,64,8,128]{4,2,3,1,0:T(8,128)} fusion(bf16[6,64,8,128]{3,2,1,0:T(8,128)(2,1)} %bitcast.63, bf16[6,64,8,128]{3,2,1,0:T(8,128)(2,1)} %bitcast.62, bf16[6,64,8,128]{3,2,1,0:T(8,128)(2,1)S(1)} %bitcast.60, f32[]{:T(128)} %bitcast.5, f32[6,64,64]{2,1,0:T(8,128)} %copy.36), kind=kOutput, calls=%fused_computation.9 | convolution fusion | flops 102236160 | bytes 4030468 | tf_op jit(solution)/shard_map/rbhpc,rbchd->rbphd/dot_general | solution.py:76
  140.9 3.5 %copy.38 = f32[1,6,64,8,128]{4,3,2,1,0:T(8,128)} copy(f32[1,6,64,8,128]{4,2,3,1,0:T(8,128)} %convolution_bitcast_fusion) | data formatting | bytes 3145728 | tf_op jit(solution)/shard_map/rbhpc,rbchd->rbphd/transpose | solution.py:76
  144.4 3.0 %copy.39 = f32[1,384,8,128]{1,3,2,0:T(8,128)} copy(f32[1,384,8,128]{3,2,1,0:T(8,128)} %bitcast.59) | data formatting | bytes 3145728 | tf_op jit(solution)/shard_map/reshape | solution.py:79
  147.4 4.3 %fusion.23 = (f32[384]{0:T(512)S(1)}, f32[1,384,8,128]{1,3,2,0:T(8,128)}) fusion(f32[1,384,8,128]{1,3,2,0:T(8,128)} %copy.39, bf16[256,8,128]{0,2,1:T(8,128)(2,1)} %bitcast.65, bf16[256,8,128]{0,2,1:T(8,128)(2,1)S(1)} %bitcast.64, f32[]{:T(128)} %bitcast.5, f32[256]{0:T(256)S(1)} %compare_convert_fusion, bf16[384,8,128]{2,1,0:T(8,128)(2,1)S(1)} %bitcast.61), kind=kOutput, calls=%fused_computation.36 | convolution fusion | flops 409730688 | bytes 4983300 | tf_op jit(solution)/shard_map/rhcn,rnhd->rchd/dot_general | solution.py:54
  151.7 1.6 multiply_reduce_fusion
  153.3 0.0 copy-start.4
  153.3 0.0 copy-start.5
  153.3 3.1 %copy.42 = f32[1,384,1024]{2,1,0:T(8,128)} copy(f32[1,384,1024]{1,2,0:T(8,128)} %bitcast.58) | data formatting | bytes 3145728 | tf_op jit(solution)/shard_map/reshape | solution.py:79
  156.5 0.0 copy-done
  156.5 0.0 copy-done.4
  156.5 0.0 copy-done.5
  156.5 3.6 %fusion.1 = bf16[1,384,1024]{2,1,0:T(8,128)(2,1)} fusion(bf16[1,384,1024]{2,1,0:T(8,128)(2,1)S(1)} %copy-done.4, bf16[1024,1024]{1,0:T(8,128)(2,1)S(1)} %copy-done, f32[1,384,1024]{2,1,0:T(8,128)} %copy.42, bf16[1,384,4096]{2,1,0:T(8,128)(2,1)} %copy-done.1, f32[1024]{0:T(1024)S(1)} %copy-done.5, f32[384]{0:T(512)S(1)} %add_sqrt_fusion, ...), kind=kOutput, calls=%fused_computation.5 | convolution fusion | flops 809238528 | bytes 6038016 | tf_op jit(solution)/shard_map/dot_general | solution.py:88
  (6 shorter events, 0.1 us)
Async XLA Ops:
  6.5 149.9 %copy-start = (bf16[1024,1024]{1,0:T(8,128)(2,1)S(1)}, bf16[1024,1024]{1,0:T(8,128)(2,1)}, u32[]{:S(2)}) copy-start(bf16[1024,1024]{1,0:T(8,128)(2,1)} %param.13) | copy-start | bytes 6291460
  6.5 4.3 %copy-start.2 = (bf16[1,128,1024]{2,1,0:T(8,128)(2,1)S(1)}, bf16[1,128,1024]{2,1,0:T(8,128)(2,1)}, u32[]{:S(2)}) copy-start(bf16[1,128,1024]{2,1,0:T(8,128)(2,1)} %param.11) | copy-start | bytes 786436
  6.5 119.2 %all-gather.2.cloned.1.call-start = ((), (), s32[]{:S(2)}) async-start(), calls=%async_computation | async-start | bytes 8912896 | tf_op jit(solution)/shard_map/all_gather | solution.py:27
  7.3 6.9 %copy-start.3 = (bf16[1,128,1024]{2,1,0:T(8,128)(2,1)S(1)}, bf16[1,128,1024]{2,1,0:T(8,128)(2,1)}, u32[]{:S(2)}) copy-start(bf16[1,128,1024]{2,1,0:T(8,128)(2,1)} %param.10) | copy-start | bytes 786436
  133.2 1.7 copy-start.1
  153.3 3.1 %copy-start.4 = (bf16[1,384,1024]{2,1,0:T(8,128)(2,1)S(1)}, bf16[1,384,1024]{2,1,0:T(8,128)(2,1)}, u32[]{:S(2)}) copy-start(bf16[1,384,1024]{2,1,0:T(8,128)(2,1)} %param.9) | copy-start | bytes 2359300
  153.3 3.1 %copy-start.5 = (f32[1024]{0:T(1024)S(1)}, f32[1024]{0:T(1024)}, u32[]{:S(2)}) copy-start(f32[1024]{0:T(1024)} %param.14) | copy-start | bytes 12292
Sparse Core Ops, SparseCore 0:
  10.1 115.5 all-gather.1
where the time goes:
time: 167 us
  waiting for transfers between devices  110 us (66%)
  matrix products  19.1 us (11%)
  local copies, waits for them, and re-layouts  15.9 us (10%)
  between operations  14.9 us (9%)
  blocking collectives  4.44 us (3%)
  other arithmetic  2.74 us (2%)
    all_gather x1, waiting for transfers between devices, on_device(): lax.all_gather(in_weight, 'req', axis=0, tiled=True)  109 us
    dot_general x1, matrix products, on_device(): jnp.dot(flat_rows, lax.all_gather(in_weight, 'req', axis=0, tiled=True),...  7.5 us
    dot_general x1, matrix products, on_device(): jnp.einsum('rhcn,rnhd->rchd', mixing, value_heads, preferred_element_type...  4.29 us
    unnamed x17, local copies, waits for them, and re-layouts  4.17 us
    dot_general x1, matrix products, on_device(): jnp.einsum('rbhpc,rbchd->rbphd', self_mix, value_blocks, preferred_elemen...  3.7 us
    dot_general x1, matrix products, on_device(): branch = jnp.dot(gated_rows, out_weight, preferred_element_type=jnp.float32)  3.6 us
    transpose x1, local copies, waits for them, and re-layouts, on_device(): jnp.einsum('rbhpc,rbchd->rbphd', self_mix, value_blocks, preferred_elemen...  3.47 us
  transfers between devices with their start and end apart: 1, of which 1 were waited for; matrix products, arithmetic and copies ran while one was open for 2% of the time, Pallas kernels for 0%

commit v1 on v0

--- a/solution.py
+++ b/solution.py
@@ -38,8 +38,13 @@
     divisor = (hist_lengths + SELF_BLOCK).astype(jnp.float32)
     cand_index = lax.axis_index("hist") * cand_count + jnp.arange(cand_count)
     is_live = cand_index[None, :] < cand_counts[:, None]
-    key_part = lax.all_gather(hist_keys, "hist", axis=1, tiled=True)
-    value_part = lax.all_gather(hist_values, "hist", axis=1, tiled=True)
+    key_part, value_part = jnp.split(
+        lax.all_gather(
+            jnp.concatenate([hist_keys, hist_values], axis=0), "hist", axis=1, tiled=True
+        ),
+        [hist_keys.shape[0]],
+        axis=0,
+    )
     span = key_part.shape[1]
     key_heads = key_part.reshape(req_count, span, HEADS, head_dim)
     value_heads = value_part.reshape(req_count, span, HEADS, head_dim)

time: 167 us -> 180 us (1.078)
  waiting for transfers between devices: 110 us -> 124 us
  blocking collectives: 4.44 us -> 0 us
  local copies, waits for them, and re-layouts: 15.9 us -> 19.1 us
    all_gather x0 -> x1, waiting for transfers between devices: none -> 8.48 us  [on_device(): lax.all_gather(jnp.concatenate([hist_keys, hist_values], axis=0), 'hist',...]
    all_gather x1, waiting for transfers between devices: 109 us -> 115 us  [on_device(): lax.all_gather(in_weight, 'req', axis=0, tiled=True)]
    all_gather x2 -> x0, blocking collectives: 4.44 us -> none  [the longest x1 2.26 us: on_device(): value_part = lax.all_gather(hist_values, 'hist', axis=1, tiled=True)]
    unnamed x17 -> x16, local copies, waits for them, and re-layouts: 4.17 us -> 6.39 us
    split x0 -> x1, local copies, waits for them, and re-layouts: none -> 2.07 us  [on_device(): jnp.split(lax.all_gather(jnp.concatenate([hist_keys, hist_values], axis=0...]
  transfers between devices with their start and end apart: 1 -> 2, of which waited for: 1 -> 2; matrix products, arithmetic and copies ran while one was open for 2% -> 2% of each run, Pallas kernels for 0% -> 0%
where the time goes in v1:
time: 180 us
  waiting for transfers between devices  124 us (69%)
  local copies, waits for them, and re-layouts  19.1 us (11%)
  matrix products  19.1 us (11%)
  between operations  14.8 us (8%)
  other arithmetic  2.7 us (2%)
    all_gather x1, waiting for transfers between devices, on_device(): lax.all_gather(in_weight, 'req', axis=0, tiled=True)  115 us
    all_gather x1, waiting for transfers between devices, on_device(): lax.all_gather(jnp.concatenate([hist_keys, hist_values], axis=0), 'hist',...  8.48 us
    dot_general x1, matrix products, on_device(): jnp.dot(flat_rows, lax.all_gather(in_weight, 'req', axis=0, tiled=True),...  7.5 us
    unnamed x16, local copies, waits for them, and re-layouts  6.39 us
    dot_general x1, matrix products, on_device(): jnp.einsum('rhcn,rnhd->rchd', mixing, value_heads, preferred_element_type...  4.29 us
    dot_general x1, matrix products, on_device(): jnp.einsum('rbhpc,rbchd->rbphd', self_mix, value_blocks, preferred_elemen...  3.7 us
  transfers between devices with their start and end apart: 2, of which 2 were waited for; matrix products, arithmetic and copies ran while one was open for 2% of the time, Pallas kernels for 0%

profile of v1, /device:TPU:0, one launch (start us, length us, event | category | flops | bytes accessed | tf_op | source)
XLA Modules:
  0.0 179.7 jit_solution(15762152119187768546)
XLA Ops:
  6.5 0.0 copy-start
  6.5 0.0 copy-start.2
  6.5 0.0 all-gather.3.cloned.1.call-start
  6.5 1.3 copy.29
  7.8 1.1 copy.30
  9.0 0.8 pad_maximum_fusion
  9.8 0.0 all-gather.3.cloned.1.call-update
  9.8 0.0 all-gather.5.cloned.1.call-start
  9.9 0.7 all-gather.5.cloned.1.call-update
  11.2 0.1 copy.35
  11.4 0.0 copy-done.2
  11.4 0.1 eq.30
  11.6 0.1 and_convert_fusion
  11.7 0.8 copy.36
  13.2 8.5 %all-gather.3.cloned.1.call-done = bf16[2,256,1024]{1,2,0:T(8,128)(2,1)} async-done(((bf16[2,128,1024]{1,2,0:T(8,128)(2,1)}), bf16[2,256,1024]{1,2,0:T(8,128)(2,1)}) %all-gather.3.cloned.1.call-update) | async-done | bytes 1048592 | tf_op jit(solution)/shard_map/all_gather | solution.py:42
  21.7 2.1 %fusion.23 = (bf16[1,256,1024]{1,2,0:T(8,128)(2,1)S(1)}, bf16[1,256,1024]{1,2,0:T(8,128)(2,1)}) fusion(bf16[2,256,1024]{1,2,0:T(8,128)(2,1)} %all-gather.3.cloned.1.call-done), kind=kLoop, calls=%fused_computation.37 | loop fusion | bytes 2097152 | tf_op jit(solution)/shard_map/split | solution.py:41
  23.7 114.8 %all-gather.5.cloned.1.call-done = bf16[1024,4096]{1,0:T(8,128)(2,1)} async-done(((bf16[64,4096]{1,0:T(8,128)(2,1)}), bf16[1024,4096]{1,0:T(8,128)(2,1)}) %all-gather.5.cloned.1.call-update) | async-done | bytes 8388624 | tf_op jit(solution)/shard_map/all_gather | solution.py:27
  138.5 7.5 %fusion = bf16[1,384,4096]{2,1,0:T(8,128)(2,1)S(1)} fusion(bf16[1024,4096]{1,0:T(8,128)(2,1)} %all-gather.5.cloned.1.call-done, bf16[1,384,1024]{2,1,0:T(8,128)(2,1)} %param.9), kind=kOutput, calls=%fused_computation.2 | convolution fusion | flops 3229089792 | bytes 12320768 | tf_op jit(solution)/shard_map/dot_general | solution.py:25
  146.0 0.0 copy-start.1
  146.0 0.5 slice_bitcast_fusion.2
  146.5 1.1 copy-done.1
  147.7 0.2 copy.43
  147.8 1.1 copy.45
  149.0 1.1 copy.46
  150.0 3.7 %convolution_bitcast_fusion = f32[1,6,64,8,128]{4,2,3,1,0:T(8,128)} fusion(bf16[6,64,8,128]{3,2,1,0:T(8,128)(2,1)} %bitcast.61, bf16[6,64,8,128]{3,2,1,0:T(8,128)(2,1)} %bitcast.60, bf16[6,64,8,128]{3,2,1,0:T(8,128)(2,1)S(1)} %bitcast.58, f32[]{:T(128)} %bitcast.6, f32[6,64,64]{2,1,0:T(8,128)} %copy.36), kind=kOutput, calls=%fused_computation.9 | convolution fusion | flops 102236160 | bytes 4030468 | tf_op jit(solution)/shard_map/rbhpc,rbchd->rbphd/dot_general | solution.py:81
  153.7 3.5 %copy.38 = f32[1,6,64,8,128]{4,3,2,1,0:T(8,128)} copy(f32[1,6,64,8,128]{4,2,3,1,0:T(8,128)} %convolution_bitcast_fusion) | data formatting | bytes 3145728 | tf_op jit(solution)/shard_map/rbhpc,rbchd->rbphd/transpose | solution.py:81
  157.2 3.0 %copy.39 = f32[1,384,8,128]{1,3,2,0:T(8,128)} copy(f32[1,384,8,128]{3,2,1,0:T(8,128)} %bitcast.57) | data formatting | bytes 3145728 | tf_op jit(solution)/shard_map/reshape | solution.py:84
  160.2 4.3 %fusion.24 = (f32[384]{0:T(512)S(1)}, f32[1,384,8,128]{1,3,2,0:T(8,128)}) fusion(f32[1,384,8,128]{1,3,2,0:T(8,128)} %copy.39, bf16[256,8,128]{0,2,1:T(8,128)(2,1)} %bitcast.63, bf16[256,8,128]{0,2,1:T(8,128)(2,1)S(1)} %bitcast.62, f32[]{:T(128)} %bitcast.6, f32[256]{0:T(256)S(1)} %compare_convert_fusion, bf16[384,8,128]{2,1,0:T(8,128)(2,1)S(1)} %bitcast.59), kind=kOutput, calls=%fused_computation.38 | convolution fusion | flops 409730688 | bytes 4983300 | tf_op jit(solution)/shard_map/rhcn,rnhd->rchd/dot_general | solution.py:59
  164.5 1.6 multiply_reduce_fusion
  166.2 0.0 copy-start.3
  166.2 0.0 copy-start.4
  166.2 3.1 %copy.42 = f32[1,384,1024]{2,1,0:T(8,128)} copy(f32[1,384,1024]{1,2,0:T(8,128)} %bitcast.56) | data formatting | bytes 3145728 | tf_op jit(solution)/shard_map/reshape | solution.py:84
  169.3 0.0 copy-done
  169.3 0.0 copy-done.3
  169.3 0.0 copy-done.4
  169.3 3.6 %fusion.1 = bf16[1,384,1024]{2,1,0:T(8,128)(2,1)} fusion(bf16[1,384,1024]{2,1,0:T(8,128)(2,1)S(1)} %copy-done.3, bf16[1024,1024]{1,0:T(8,128)(2,1)S(1)} %copy-done, f32[1,384,1024]{2,1,0:T(8,128)} %copy.42, bf16[1,384,4096]{2,1,0:T(8,128)(2,1)} %copy-done.1, f32[1024]{0:T(1024)S(1)} %copy-done.4, f32[384]{0:T(512)S(1)} %add_sqrt_fusion, ...), kind=kOutput, calls=%fused_computation.5 | convolution fusion | flops 809238528 | bytes 6038016 | tf_op jit(solution)/shard_map/dot_general | solution.py:93
  (7 shorter events, 0.1 us)
Async XLA Ops:
  6.5 162.8 %copy-start = (bf16[1024,1024]{1,0:T(8,128)(2,1)S(1)}, bf16[1024,1024]{1,0:T(8,128)(2,1)}, u32[]{:S(2)}) copy-start(bf16[1024,1024]{1,0:T(8,128)(2,1)} %param.13) | copy-start | bytes 6291460
  6.5 4.8 %copy-start.2 = (s32[1,384,64]{1,2,0:T(8,128)S(1)}, s32[1,384,64]{1,2,0:T(8,128)}, u32[]{:S(2)}) copy-start(s32[1,384,64]{1,2,0:T(8,128)} %param.17) | copy-start | bytes 294916
  6.5 15.1 %all-gather.3.cloned.1.call-start = ((), (), s32[]{:S(2)}) async-start(), calls=%async_computation | async-start | bytes 1572864 | tf_op jit(solution)/shard_map/all_gather | solution.py:42
  9.8 128.7 %all-gather.5.cloned.1.call-start = ((), (), s32[]{:S(2)}) async-start(), calls=%async_computation.1 | async-start | bytes 8912896 | tf_op jit(solution)/shard_map/all_gather | solution.py:27
  146.0 1.6 copy-start.1
  166.2 3.1 %copy-start.3 = (bf16[1,384,1024]{2,1,0:T(8,128)(2,1)S(1)}, bf16[1,384,1024]{2,1,0:T(8,128)(2,1)}, u32[]{:S(2)}) copy-start(bf16[1,384,1024]{2,1,0:T(8,128)(2,1)} %param.9) | copy-start | bytes 2359300
  166.2 3.1 %copy-start.4 = (f32[1024]{0:T(1024)S(1)}, f32[1024]{0:T(1024)}, u32[]{:S(2)}) copy-start(f32[1024]{0:T(1024)} %param.14) | copy-start | bytes 12292
Sparse Core Ops, SparseCore 0:
  9.9 11.6 all-gather.2
  24.4 114.0 all-gather.4
